TPU v7x, 256 devices: a whole 4x4x8 slice. The times are simulated.
256 devices in a mesh: row: 16 (over z_hi, x, core), col: 16 (over y, z_lo).
Axes of the slice: x: 4, y: 4, z: 8 (z_hi: 2, z_lo: 4; z = z_hi * 4 + z_lo), core: 2. Of those that a mesh axis runs over, the one named last changes fastest.
Arguments:
- latent: bfloat16 [1280, 64, 128], P('row', 'col'), may hold values from -100 to 100
- stale_act: bfloat16 [1280, 64, 128], P('row', 'col'), may hold values from -6 to 6
- stale_kv: bfloat16 [2, 1280, 64, 128], P(None, None, 'col'), may hold values from -400 to 400
- gn_gain: float32 [1280], P('row'), may hold values from 0.5 to 1.5
- gn_bias: float32 [1280], P('row'), may hold values from -3 to 3
- temb: float32 [1280], P('row'), may hold values from -4 to 4
- conv_w: bfloat16 [3, 3, 1280, 1280], P(None, None, 'row'), may hold values from -0.3125 to 0.3125
- w_qkv: bfloat16 [1280, 3, 1280], P('row'), may hold values from -0.15625 to 0.15625
Outputs:
- hidden: bfloat16 [1280, 64, 128], P('row', 'col')
- attn: bfloat16 [512, 64, 320], P('row', 'col')
All inputs are finite; a program needn't handle non-finite values.
Results may differ from a plain program's by a relative error of at most 0.024.
Values may be sent and summed in bfloat16 or wider, within the bound.
A program may use at most 128 MiB of HBM per device.

v0:
```python
from functools import partial
import math

import jax
import jax.numpy as jnp
from jax import lax
from jax.sharding import PartitionSpec as P

D = 1280
HEAD = 64
HGROUPS = 4
GROUPS = 32


EPS = 1e-05
NEG = -1e30


def with_halo(cells, sides, width):
    for axis, dim in sides:
        count = lax.axis_size(axis)
        ends = count - 1
        head = lax.slice_in_dim(cells, 0, width, axis=dim)
        tail = lax.slice_in_dim(cells, cells.shape[dim] - width, cells.shape[dim], axis=dim)
        cells = jnp.concatenate(
            [
                lax.ppermute(tail, axis, [(i, (i + 1) % count) for i in range(ends)]),
                cells,
                lax.ppermute(head, axis, [((i + 1) % count, i) for i in range(ends)]),
            ],
            axis=dim,
        )
    return cells


def attend_block(carry, keys, values, query, allowed):
    best, total, accum = carry
    scale = query.shape[1] ** (-0.5)
    scores = jnp.einsum("hdk,hdq->hkq", keys, query, preferred_element_type=jnp.float32) * scale
    scores = jnp.where(allowed[None, :, None], scores, NEG)
    top = jnp.maximum(best, jnp.max(scores, axis=1))
    keep = jnp.exp(best - top)
    probs = jnp.exp(scores - top[:, None, :])
    total = total * keep + jnp.sum(probs, axis=1)
    accum = accum * keep[:, None, :] + jnp.einsum(
        "hkq,hdk->hdq", probs.astype(jnp.bfloat16), values, preferred_element_type=jnp.float32
    )
    return (top, total, accum)


def attend_piece(carry, piece, start, query, own_band, band_cols):
    ncols = piece.shape[2]
    rows = piece.shape[3]
    heads_loc = query.shape[0]
    head = query.shape[1]
    width = math.gcd(ncols, band_cols)

    def one_block(index, state):
        sub = lax.dynamic_slice_in_dim(piece, index * width, width, 2)
        flat = sub.reshape(2, heads_loc, head, width * rows)
        column = index * width + jnp.arange(width, dtype=jnp.int32)
        allowed = jnp.broadcast_to(
            (column // band_cols != own_band)[:, None], (width, rows)
        ).reshape(-1)
        return attend_block(state, flat[0], flat[1], query, allowed)

    return lax.fori_loop(0, ncols // width, one_block, carry)


def on_device(latent, stale_act, stale_kv, gn_gain, gn_bias, temb, conv_w, w_qkv):
    chans, cols, rows = latent.shape
    tokens = cols * rows
    row_parts = lax.axis_size("row") // HGROUPS
    row_index = lax.axis_index("row")
    head_group = row_index // row_parts
    row_part = row_index % row_parts
    qrows = rows // row_parts
    gchans = D // HGROUPS
    qtokens = cols * qrows
    stale_mine = lax.dynamic_slice_in_dim(stale_kv, head_group * gchans, gchans, 1)
    xf = latent.astype(jnp.float32)
    group = D // GROUPS
    grouped = xf.reshape(chans // group, group * tokens)
    count = group * tokens * lax.axis_size("col")
    gmean = lax.psum(jnp.sum(grouped, axis=1), "col") / count
    centred = grouped - gmean[:, None]
    gvar = lax.psum(jnp.sum(centred * centred, axis=1), "col") / count
    normed = (centred * lax.rsqrt(gvar + EPS)[:, None]).reshape(chans, cols, rows)
    act = jax.nn.silu(normed * gn_gain[:, None, None] + gn_bias[:, None, None]).astype(jnp.bfloat16)
    border = with_halo(stale_act, (("col", 1),), 1)
    block = jnp.concatenate([border[:, :1], act, border[:, -1:]], axis=1)
    block = jnp.pad(block, ((0, 0), (0, 0), (1, 1)))
    shifted = [
        block[:, sw : sw + cols, sh : sh + rows].reshape(chans, tokens)
        for sw in range(3)
        for sh in range(3)
    ]
    total = jnp.zeros((lax.axis_size("row") * chans, tokens), jnp.float32)
    for offset in range(9):
        w_slice = conv_w[offset // 3, offset % 3]
        total = total + lax.dot_general(
            w_slice, shifted[offset], (((0,), (0,)), ((), ())), preferred_element_type=jnp.float32
        )
    conv = lax.psum_scatter(total, "row", scatter_dimension=0, tiled=True)
    hidden = (xf.reshape(chans, tokens) + conv + temb[:, None]).astype(jnp.bfloat16)
    hpiece = lax.all_gather(hidden, "row", axis=0, tiled=True)
    wpiece = lax.all_gather(w_qkv, "row", axis=0, tiled=True)
    depth = hpiece.shape[0]
    wsel = lax.dynamic_slice_in_dim(wpiece, head_group * gchans, gchans, 2)
    w_query = wsel[:, 0]
    w_keyval = wsel[:, 1:].reshape(depth, 2 * gchans)
    qpiece = lax.dynamic_slice_in_dim(
        hpiece.reshape(depth, cols, rows), row_part * qrows, qrows, 2
    ).reshape(depth, qtokens)
    qproj = lax.dot_general(
        w_query, qpiece, (((0,), (0,)), ((), ())), preferred_element_type=jnp.float32
    )
    kvproj = lax.dot_general(
        w_keyval, hpiece, (((0,), (0,)), ((), ())), preferred_element_type=jnp.float32
    )
    pf = hpiece.astype(jnp.float32)
    colsum = jnp.sum(wsel.astype(jnp.float32), axis=0).reshape(3 * gchans)
    qproj, kvproj, first, second, colsum = (
        qproj,
        kvproj,
        jnp.sum(pf, axis=0),
        jnp.sum(pf * pf, axis=0),
        colsum,
    )
    mu = first / D
    rstd = lax.rsqrt(second / D - mu * mu + EPS)
    mu_query = lax.dynamic_slice_in_dim(mu.reshape(cols, rows), row_part * qrows, qrows, 1).reshape(
        qtokens
    )
    rstd_query = lax.dynamic_slice_in_dim(
        rstd.reshape(cols, rows), row_part * qrows, qrows, 1
    ).reshape(qtokens)
    heads_loc = gchans // HEAD
    query = ((qproj - colsum[:gchans, None] * mu_query[None, :]) * rstd_query[None, :]).astype(
        jnp.bfloat16
    )
    query = query.reshape(heads_loc, HEAD, qtokens)
    keyval = ((kvproj - colsum[gchans:, None] * mu[None, :]) * rstd[None, :]).astype(jnp.bfloat16)
    keyval = keyval.reshape(2, heads_loc, HEAD, tokens)
    carry = (
        jnp.full((heads_loc, qtokens), NEG, jnp.float32),
        jnp.zeros((heads_loc, qtokens), jnp.float32),
        jnp.zeros((heads_loc, HEAD, qtokens), jnp.float32),
    )
    carry = attend_block(carry, keyval[0], keyval[1], query, jnp.ones((tokens,), bool))
    own_band = lax.axis_index("col")
    folder = partial(attend_piece, query=query, own_band=own_band, band_cols=cols)
    carry = folder(carry, lax.all_gather(stale_mine, "col", axis=2, tiled=True), jnp.int32(0))
    best, total, accum = carry
    attn = (
        (accum / total[:, None, :])
        .reshape(gchans, cols, qrows)
        .transpose(2, 1, 0)
        .astype(jnp.bfloat16)
    )
    return (hidden.reshape(chans, cols, rows), attn)


def solution(mesh):
    return jax.shard_map(
        on_device,
        mesh=mesh,
        in_specs=(
            P("row", "col", None),
            P("row", "col", None),
            P(None, None, "col", None),
            P("row"),
            P("row"),
            P("row"),
            P(None, None, "row", None),
            P("row", None, None),
        ),
        out_specs=(P("row", "col", None), P("row", "col", None)),
        check_vma=False,
    )
```

profile of v0, /device:TPU:1, one launch (start us, length us, event | category | flops | bytes accessed | tf_op | source)
XLA Modules:
  0.0 663.2 jit_solution(7207997589130689993)
XLA Ops:
  7.2 1.2 fusion.69
  8.4 1.6 convert_reduce_fusion.2
  10.1 1.3 collective-permute-start.1
  11.4 39.5 %psum.14 = f32[2]{0:T(128)S(1)} all-reduce(f32[2]{0:T(128)S(1)} %reduce_sum.86), channel_id=1, replica_groups=mesh['row'=16,'col'=16] {'col'}, use_global_device_ids=true, to_apply=%region_2.3 | all-reduce | flops 2 | bytes 16 | tf_op jit(solution)/shard_map/psum | solution.py:85
  51.1 2.1 multiply_reduce_fusion
  53.3 1.3 collective-permute-start
  54.6 31.2 %psum.15 = f32[2]{0:T(128)S(1)} all-reduce(f32[2]{0:T(128)S(1)} %reduce_sum.89), channel_id=1, replica_groups=mesh['row'=16,'col'=16] {'col'}, use_global_device_ids=true, to_apply=%region_5.6 | all-reduce | flops 2 | bytes 16 | tf_op jit(solution)/shard_map/psum | solution.py:87
  86.0 1.3 fusion.43
  88.1 1.6 fusion.32
  93.6 2.1 fusion.6
  95.7 3.2 copy.34
  99.9 102.3 %reduce-scatter.4.cloned.1.call-done = f32[80,512]{1,0:T(8,128)} async-done(((f32[1280,512]{1,0:T(8,128)}), f32[80,512]{1,0:T(8,128)}) %reduce-scatter.4.cloned.1.call-update) | async-done | bytes 163856
  207.1 54.3 %all-gather.6.cloned.1.call-done = bf16[1280,512]{1,0:T(8,128)(2,1)} async-done(((bf16[80,512]{1,0:T(8,128)(2,1)}), bf16[1280,512]{1,0:T(8,128)(2,1)}) %all-gather.6.cloned.1.call-update) | async-done | bytes 1310736 | tf_op jit(solution)/shard_map/all_gather | solution.py:106
  261.4 1.8 convert_reduce_fusion.1
  264.1 115.5 %all-gather.4.cloned.1.call-done = bf16[1280,3,1280]{2,0,1:T(8,128)(2,1)} async-done(((bf16[80,3,1280]{2,0,1:T(8,128)(2,1)}), bf16[1280,3,1280]{2,0,1:T(8,128)(2,1)}) %all-gather.4.cloned.1.call-update) | async-done | bytes 9830416 | tf_op jit(solution)/shard_map/all_gather | solution.py:107
  379.6 5.4 constant_dynamic-slice_fusion.6
  385.0 4.0 copy.38
  389.0 1.3 slice.138
  390.8 2.8 fusion.9
  395.0 210.3 %all-gather.8.cloned.1.call-done = bf16[2,320,64,128]{3,1,0,2:T(8,128)(2,1)} async-done(((bf16[2,320,4,128]{3,1,0,2:T(8,128)(2,1)}), bf16[2,320,64,128]{3,1,0,2:T(8,128)(2,1)}) %all-gather.8.cloned.1.call-update) | async-done | bytes 10485776 | tf_op jit(solution)/shard_map/all_gather | solution.py:153
  605.3 49.6 %while.19 = (s32[]{:T(128)}, f32[5,128]{1,0:T(8,128)S(1)}, f32[5,128]{1,0:T(8,128)S(1)}, f32[5,64,128]{2,1,0:T(8,128)S(1)}, s32[]{:T(128)}, /*index=5*/bf16[2,32...) while((s32[]{:T(128)}, f32[5,128]{1,0:T(8,128)S(1)}, ...), condition=%wide.region_15.16_spmd, body=%wide.region_12.15_spmd.sunk | while | flops 86263112 | bytes 8971471 | solution.py:67
  614.6 1.1 constant_dynamic-slice_fusion.8
  623.9 1.1 constant_dynamic-slice_fusion.8
  630.1 1.1 constant_dynamic-slice_fusion.8
  (276 shorter events, 60.4 us)
Async XLA Ops:
  7.2 197.9 %copy-start = (bf16[2,1280,4,128]{3,2,1,0:T(4,128)(2,1)S(1)}, bf16[2,1280,4,128]{3,2,1,0:T(4,128)(2,1)}, u32[]{:S(2)}) copy-start(bf16[2,1280,4,128]{3,2,1,0:T(4,128)(2,1)} %param.12) | copy-start | bytes 7864324
  7.2 195.0 %reduce-scatter.4.cloned.1.call-start = ((), (), s32[]{:S(2)}) async-start(), calls=%async_computation.4 | async-start | bytes 2785280
  10.1 77.1 %collective-permute-start.1 = (bf16[80,1,128]{2,1,0:T(2,128)(2,1)S(1)}, bf16[80,1,128]{2,1,0:T(2,128)(2,1)S(1)}, u32[]{:S(2)}, u32[]{:S(2)}) collective-permute-start(bf16[80,1,128]{2,1,0:T(2,128)(2,1)S(1)} %get-tuple-element.237), channel_id=1, source_target_pairs={{1,0},{2,1},{3,2},{4,3},{5,4},{6,5},{7,6},{8,7},{9,8},{10,9},{11,1... | collective-permute-start | bytes 61448 | tf_op jit(solution)/shard_map/ppermute | solution.py:29
  53.3 34.0 %collective-permute-start = (bf16[80,1,128]{2,1,0:T(2,128)(2,1)S(1)}, bf16[80,1,128]{2,1,0:T(2,128)(2,1)S(1)}, u32[]{:S(2)}, u32[]{:S(2)}) collective-permute-start(bf16[80,1,128]{2,1,0:T(2,128)(2,1)S(1)} %get-tuple-element.236), channel_id=1, source_target_pairs={{0,1},{1,2},{2,3},{3,4},{4,5},{5,6},{6,7},{7,8},{8,9},{9,10},{10,1... | collective-permute-start | bytes 61448 | tf_op jit(solution)/shard_map/ppermute | solution.py:27
  88.1 1.8 copy-start.3
  98.9 0.9 copy-start.4
  98.9 104.3 %copy-start.5 = (f32[80]{0:T(128)S(1)}, f32[80]{0:T(128)}, u32[]{:S(2)}) copy-start(f32[80]{0:T(128)} %param.15) | copy-start | bytes 964
  98.9 162.4 %all-gather.6.cloned.1.call-start = ((), (), s32[]{:S(2)}) async-start(), calls=%async_computation.2 | async-start | bytes 1392640 | tf_op jit(solution)/shard_map/all_gather | solution.py:106
  204.0 175.6 %all-gather.4.cloned.1.call-start = ((), (), s32[]{:S(2)}) async-start(), calls=%async_computation.1 | async-start | bytes 10444800 | tf_op jit(solution)/shard_map/all_gather | solution.py:107
  204.8 400.5 %all-gather.8.cloned.1.call-start = ((), (), s32[]{:S(2)}) async-start(), calls=%async_computation.3 | async-start | bytes 11141120 | tf_op jit(solution)/shard_map/all_gather | solution.py:153
  261.4 2.1 copy-start.2
  654.9 1.8 copy-start.1
Sparse Core Ops, SparseCore 0:
  99.0 103.0 reduce-scatter.3
  205.8 55.4 all-gather.5
  264.5 115.0 all-gather.3
  381.4 223.8 all-gather.7
where the time goes:
time: 664 us; the launch traced here: 663 us
  waiting for transfers between devices  483 us (73%)
  blocking collectives  70.6 us (11%)
  local copies, waits for them, and re-layouts  54.8 us (8%)
  matrix products  24.3 us (4%)
  between operations  14.1 us (2%)
  other arithmetic  11.9 us (2%)
    all_gather x1, waiting for transfers between devices, on_device(): lax.all_gather(stale_mine, 'col', axis=2, tiled=True)  210 us
    all_gather x1, waiting for transfers between devices, on_device(): wpiece = lax.all_gather(w_qkv, 'row', axis=0, tiled=True)  115 us
    unnamed x5, waiting for transfers between devices  103 us
    all_gather x1, waiting for transfers between devices, on_device(): hpiece = lax.all_gather(hidden, 'row', axis=0, tiled=True)  54.3 us
    psum x1, blocking collectives, on_device(): gmean = lax.psum(jnp.sum(grouped, axis=1), 'col') / count  39.5 us
    psum x1, blocking collectives, on_device(): gvar = lax.psum(jnp.sum(centred * centred, axis=1), 'col') / count  31.2 us
    slice x16, local copies, waits for them, and re-layouts, one_block(): return attend_block(state, flat[0], flat[1], query, allowed)  18 us
  transfers between devices with their start and end apart: 6, of which 4 were waited for; matrix products, arithmetic and copies ran while one was open for 4% of the time, Pallas kernels for 0%

commit v1 on v0

v1 whole, which is shorter than its diff:
```python
import itertools
import math

import jax
import jax.numpy as jnp
from jax import lax
from jax.experimental import pallas as pl
from jax.experimental.pallas import tpu as pltpu
from jax.sharding import PartitionSpec as P

D = 1280
HEAD = 64
HGROUPS = 4
GROUPS = 32
EPS = 1e-05

F32 = jnp.float32
BF16 = jnp.bfloat16
MESH = pl.DeviceIdType.MESH

CH = 80
GC = 320
NHEAD = 5
COLS = 4
ROWS = 128
TOK = COLS * ROWS
QT = 128
NSEM = 80


def dot(a, b, ca, cb):
    return lax.dot_general(a, b, (((ca,), (cb,)), ((), ())), preferred_element_type=F32)


def as_column(row):
    n = row.shape[1]
    r = lax.broadcasted_iota(jnp.int32, (n, n), 0)
    c = lax.broadcasted_iota(jnp.int32, (n, n), 1)
    return jnp.sum(jnp.where(r == c, jnp.broadcast_to(row, (n, n)), 0.0), axis=1, keepdims=True)


def kernel(
    lat_ref, edge_ref, kv_hbm, gain_ref, bias_ref, temb_ref, cw_hbm, w_ref,
    hid_ref, attn_ref,
    cw, wsrc, wt, wtsib, x3, x3sib, halo, st_a, st_all, pb, rx, zs, zr,
    hall, wz, wg, kb, kf, qx, qpeer, oown, oret, oback, lret, lback, lses,
    ss, rs, ls,
):
    row = lax.axis_index("row")
    col = lax.axis_index("col")
    zh, x, k = row // 8, (row // 2) % 4, row % 2
    y, zl = col // 4, col % 4
    group = row // 4
    part = row % 4
    ids = itertools.count()

    def at_row(zh_, x_, k_):
        return zh_ * 8 + x_ * 2 + k_

    def dev(r, c):
        return (r, c)

    sib = dev(at_row(zh, x, 1 - k), col)
    wpeer = (at_row(1 - zh, x, k), y * 4 + 3 - zl)
    zpeer = dev(at_row(1 - zh, x, k), col)
    xs = {d: (x + d) % 4 for d in (1, 2, 3)}
    xpeer = {d: dev(at_row(zh, xs[d], k), col) for d in (1, 2, 3)}
    ypeer = {d: dev(row, ((y + d) % 4) * 4 + zl) for d in (1, 2, 3)}
    lpeer = {d: dev(row, y * 4 + (zl + d) % 4) for d in (1, 2, 3)}
    nxt = dev(row, (col + 1) % 16)
    prv = dev(row, (col + 15) % 16)
    flip = zl + 1 - 2 * (zl % 2)
    near = dev(row, y * 4 + flip)
    qpartner = lpeer[2]
    others = {
        (dy, dz): dev(row, ((y + dy) % 4) * 4 + (zl + dz) % 4)
        for dy in range(4) for dz in range(4) if dy or dz
    }
    r_z = at_row(1 - zh, x, k)

    started = []

    def rcopy(src, dst, to):
        i = next(ids)
        cp = pltpu.make_async_remote_copy(
            src_ref=src, dst_ref=dst, send_sem=ss.at[i], recv_sem=rs.at[i],
            device_id=to, device_id_type=MESH,
        )
        cp.start()
        started.append(cp)
        return cp

    lc_w = pltpu.make_async_copy(cw_hbm, cw, ls.at[0])
    lc_w.start()
    lc_kv = pltpu.make_async_copy(kv_hbm, kb.at[:, 0], ls.at[1])
    lc_kv.start()

    bar = pltpu.get_barrier_semaphore()
    peers = [sib, zpeer, wpeer, *xpeer.values(), *others.values(), nxt, prv]
    for p in peers:
        pl.semaphore_signal(bar, inc=1, device_id=p, device_id_type=MESH)

    for i in range(3):
        part_w = w_ref[i]
        for g in range(HGROUPS):
            wsrc[g, :, i * GC:(i + 1) * GC] = part_w[:, g * GC:(g + 1) * GC]
    lc_own = pltpu.make_async_copy(wsrc.at[group], wg.at[row], ls.at[2])
    lc_own.start()

    xf = lat_ref[...].astype(F32)
    n_loc = 40 * TOK
    halves = [xf[0:40], xf[40:80]]
    means = [jnp.sum(jnp.sum(h, axis=1, keepdims=True), axis=0, keepdims=True) / n_loc for h in halves]
    m2s = [
        jnp.sum(jnp.sum((h - m) * (h - m), axis=1, keepdims=True), axis=0, keepdims=True)
        for h, m in zip(halves, means)
    ]
    rid = lax.broadcasted_iota(jnp.int32, (8, 128), 0)
    tile = jnp.zeros((8, 128), F32)
    for i, v in enumerate(means + m2s):
        tile = jnp.where(rid == i, jnp.broadcast_to(v, (8, 128)), tile)
    st_a[...] = tile

    pl.semaphore_wait(bar, len(peers))

    c_st = [
        rcopy(st_a, st_all.at[dy * 4 + dz - 1], to) for (dy, dz), to in others.items()
    ]
    c_halo_n = rcopy(edge_ref.at[1], halo.at[0], nxt)
    c_halo_p = rcopy(edge_ref.at[0], halo.at[1], prv)

    c_wx = {d: rcopy(wsrc.at[zh * 2 + xs[d] // 2], wg.at[row], xpeer[d]) for d in (1, 2, 3)}
    c_ws = rcopy(wsrc.at[group], wg.at[row], sib)
    lc_w.wait()
    eye = (
        lax.broadcasted_iota(jnp.int32, (128, 128), 0) == lax.broadcasted_iota(jnp.int32, (128, 128), 1)
    ).astype(BF16)

    def flip_weights(a):
        for half in range(2):
            blocks = [
                dot(eye, cw[a, :, (half * 5 + i) * 128:(half * 5 + i + 1) * 128], 1, 1).astype(BF16)
                for i in range(5)
            ]
            wt[a, half] = jnp.concatenate(blocks, axis=0).reshape(4, 2, CH, 240)

    flip_weights(0)

    flip_weights(1)
    flip_weights(2)
    c_wt = rcopy(wt.at[:, :, :, 1 - k], wtsib, sib)

    lane = lax.broadcasted_iota(jnp.int32, (CH, ROWS), 1)

    def shifts(colv):
        left = jnp.where(lane == 0, 0.0, pltpu.roll(colv, 1, axis=1))
        right = jnp.where(lane == ROWS - 1, 0.0, pltpu.roll(colv, ROWS - 1, axis=1))
        return [left.astype(BF16), colv.astype(BF16), right.astype(BF16)]

    def put_column(slot, colv):
        for c, v in enumerate(shifts(colv)):
            x3[c * CH:(c + 1) * CH, slot * ROWS:(slot + 1) * ROWS] = v

    gain = as_column(gain_ref[...])
    bias = as_column(bias_ref[...])
    temb = as_column(temb_ref[...])

    c_halo_n.wait_recv()
    c_halo_p.wait_recv()
    put_column(0, jnp.where(col > 0, halo[0].astype(F32), 0.0))
    put_column(5, jnp.where(col < 15, halo[1].astype(F32), 0.0))

    for c in c_st:
        c.wait_recv()
    tiles = [tile] + [st_all[i] for i in range(15)]
    gmean = sum(t[0:2] for t in tiles) / 16.0
    gm2 = sum(t[2:4] for t in tiles)
    for t in tiles:
        dlt = t[0:2] - gmean
        gm2 = gm2 + float(n_loc) * dlt * dlt
    ginv = lax.rsqrt(gm2 / float(16 * n_loc) + EPS)
    c_near = rcopy(kv_hbm.at[k], kb.at[k, 4], near)
    c_wz = rcopy(wsrc.at[pl.ds(2 * (1 - zh), 2)], wz, wpeer)
    c_kvy = {d: rcopy(kv_hbm.at[k], kb.at[k, d], ypeer[d]) for d in (1, 2, 3)}
    mean_c = jnp.concatenate(
        [jnp.broadcast_to(gmean[0:1], (40, 128)), jnp.broadcast_to(gmean[1:2], (40, 128))], axis=0
    )
    inv_c = jnp.concatenate(
        [jnp.broadcast_to(ginv[0:1], (40, 128)), jnp.broadcast_to(ginv[1:2], (40, 128))], axis=0
    )
    for w in range(COLS):
        v = (xf[:, w * ROWS:(w + 1) * ROWS] - mean_c) * inv_c * gain + bias
        act = v / (1.0 + jnp.exp(-v))
        put_column(1 + w, act.astype(BF16).astype(F32))
    c_x3 = rcopy(x3, x3sib, sib)

    c_wt.wait_recv()
    c_x3.wait_recv()
    c_rx = []
    for half in range(2):
        zz = (1 - zh) if half == 0 else zh
        acc = jnp.zeros((4 * CH, TOK), F32)
        for a in range(3):
            acc = acc + dot(
                wt[a, zz, :, k].reshape(4 * CH, 240), x3[:, a * ROWS:a * ROWS + TOK], 1, 0
            )
        for a in range(3):
            acc = acc + dot(
                wtsib[a, zz].reshape(4 * CH, 240), x3sib[:, a * ROWS:a * ROWS + TOK], 1, 0
            )
        pb[half] = acc.astype(BF16).reshape(4, CH, TOK)
        c_rx.append([rcopy(pb.at[half, xs[d]], rx.at[half, d - 1], xpeer[d]) for d in (1, 2, 3)])

    def keys_second():
        c_near.wait_recv()
        ks = [rcopy(kb.at[k, 4], kb.at[k, 4], sib)]
        return {d: rcopy(kb.at[k, 4], kb.at[k, 4 + d], ypeer[d]) for d in (1, 2, 3)}, ks

    def weights_second():
        mine = x // 2
        c_wz.wait_recv()
        lc = pltpu.make_async_copy(wz.at[mine], wg.at[r_z], ls.at[3])
        lc.start()
        cx = {d: rcopy(wz.at[xs[d] // 2], wg.at[r_z], xpeer[d]) for d in (1, 2, 3)}
        return lc, cx, rcopy(wz.at[mine], wg.at[r_z], sib)

    sums = []
    for half in range(2):
        for c in c_rx[half]:
            c.wait_recv()
        total = pb[half, x].astype(F32)
        for d in range(3):
            total = total + rx[half, d].astype(F32)
        if half == 0:
            zs[...] = total.astype(BF16)
            c_zr = rcopy(zs, zr, zpeer)
        sums.append(total)

    c_kvy2, c_ks = keys_second()
    lc_z, c_wx2, c_ws2 = weights_second()

    c_zr.wait_recv()
    hid = (xf + (sums[1] + zr[...].astype(F32)) + temb).astype(BF16)
    hid_ref[...] = hid
    hall[row] = hid

    c_hz = rcopy(hall.at[row], hall.at[row], zpeer)
    c_hx = {d: rcopy(hall.at[row], hall.at[row], xpeer[d]) for d in (1, 2, 3)}
    c_hs = [rcopy(hall.at[row], hall.at[row], sib)]
    c_hz.wait_recv()
    c_hx2 = {d: rcopy(hall.at[r_z], hall.at[r_z], xpeer[d]) for d in (1, 2, 3)}
    c_hs.append(rcopy(hall.at[r_z], hall.at[r_z], sib))

    w_fwd = []
    for d in (1, 2, 3):
        src = at_row(zh, (x + 4 - d) % 4, k)
        c_wx[d].wait_recv()
        w_fwd.append(rcopy(wg.at[src], wg.at[src], sib))
        c_kvy[d].wait_recv()
        c_ks.append(rcopy(kb.at[k, d], kb.at[k, d], sib))
    for leg, cs in ((0, c_hx), (1, c_hx2)):
        for d in (1, 2, 3):
            src = at_row(zh if leg == 0 else 1 - zh, (x + 4 - d) % 4, k)
            cs[d].wait_recv()
            c_hs.append(rcopy(hall.at[src], hall.at[src], sib))
    for d in (1, 2, 3):
        src = at_row(1 - zh, (x + 4 - d) % 4, k)
        c_wx2[d].wait_recv()
        w_fwd.append(rcopy(wg.at[src], wg.at[src], sib))

    c_kfwd = []
    for d in (1, 2, 3):
        c_kvy2[d].wait_recv()
        c_kfwd.append(rcopy(kb.at[k, 4 + d], kb.at[k, 4 + d], sib))

    lc_own.wait()
    lc_z.wait()
    for c in [c_ws, c_ws2, *w_fwd]:
        c.wait_recv()
    wfull = wg[...].reshape(D, 3 * GC)
    colsum = dot(wfull, jnp.ones((D, 128), BF16), 0, 0)
    for c in c_hs:
        c.wait_recv()

    hfull = hall[...].reshape(D, TOK)
    hf = hfull.astype(F32)
    mu = jnp.sum(hf, axis=0, keepdims=True) / D
    nvar = jnp.sum(hf * hf, axis=0, keepdims=True) / D - mu * mu
    rstd = lax.rsqrt(nvar + EPS)
    proj = dot(wfull, hfull, 0, 0)
    qkv = (proj - colsum[:, 0:1] * mu) * rstd
    qcm = (qkv[0:GC] * (HEAD ** -0.5 * math.log2(math.e))).astype(BF16)
    kf[0] = qkv[GC:2 * GC].astype(BF16)
    kf[1] = qkv[2 * GC:].astype(BF16)

    qi = lax.broadcasted_iota(jnp.int32, (QT, TOK), 0)
    ti = lax.broadcasted_iota(jnp.int32, (QT, TOK), 1)
    pick = (ti == (qi & 3) * ROWS + part * 32 + (qi >> 2)).astype(BF16)
    qtm = dot(pick, qcm, 1, 1).astype(BF16)
    qx[...] = qtm
    c_q = rcopy(qx, qpeer, qpartner)

    lc_kv.wait()
    for c in c_ks + c_kfwd:
        c.wait_recv()

    def head_rows(h):
        return pl.ds(h * HEAD, HEAD)

    def keys_of(h, own):
        first = kf[0, head_rows(h), :] if own else kb[0, 0, head_rows(h), :]
        return [first] + [kb[0, i, head_rows(h), :] for i in range(1, 8)]

    def values_of(h, own):
        first = kf[1, head_rows(h), :] if own else kb[1, 0, head_rows(h), :]
        return [first] + [kb[1, i, head_rows(h), :] for i in range(1, 8)]

    def weigh(scores, best, values):
        out = jnp.zeros((QT, HEAD + 16), F32)
        for s, v in zip(scores, values):
            p = jnp.exp2(s - best).astype(BF16)
            out = out + dot(p, jnp.concatenate([v, jnp.ones((16, TOK), BF16)], axis=0), 1, 1)
        norm = out[:, HEAD:HEAD + 1]
        return out[:, 0:HEAD] / norm, best + jnp.log2(norm)

    diag = lax.broadcasted_iota(jnp.int32, (QT, QT), 0) == lax.broadcasted_iota(jnp.int32, (QT, QT), 1)
    c_o = []

    def finish(h, own, scores, best):
        o, lse = weigh(scores, best, values_of(h, own))
        if own:
            oown[h] = o
            lses[h] = jnp.broadcast_to(lse, (QT, 128))
            return
        oret[h // 2, :, (h % 2) * HEAD:(h % 2 + 1) * HEAD] = o.astype(BF16)
        lret[h:h + 1] = jnp.sum(
            jnp.where(diag, jnp.broadcast_to(lse, (QT, QT)), 0.0), axis=0, keepdims=True
        )
        if h % 2 == 1:
            c_o.append(rcopy(oret.at[h // 2], oback.at[h // 2], qpartner))

    lret[...] = jnp.zeros((8, 128), F32)
    oret[2, :, HEAD:128] = jnp.zeros((QT, HEAD), BF16)
    held = None
    for own in (True, False):
        if not own:
            c_q.wait_recv()
        q_all = qtm if own else qpeer[...]
        for h in range(NHEAD):
            q = q_all[:, h * HEAD:(h + 1) * HEAD]
            scores = [dot(q, kk, 1, 0) for kk in keys_of(h, own)]
            top = scores[0]
            for sc in scores[1:]:
                top = jnp.maximum(top, sc)
            best = jnp.max(top, axis=1, keepdims=True)
            if held is not None:
                finish(*held)
            held = (h, own, scores, best)
    finish(*held)
    c_o.append(rcopy(oret.at[2], oback.at[2], qpartner))
    c_o.append(rcopy(lret, lback, qpartner))
    for c in c_o:
        c.wait_recv()

    outs = []
    for h in range(NHEAD):
        o1 = oback[h // 2, :, (h % 2) * HEAD:(h % 2 + 1) * HEAD].astype(F32)
        lse1 = as_column(lback[h:h + 1])
        lse0 = lses[h][:, 0:1]
        top = jnp.maximum(lse0, lse1)
        w0 = jnp.exp2(lse0 - top)
        w1 = jnp.exp2(lse1 - top)
        outs.append((oown[h] * w0 + o1 * w1) / (w0 + w1))
    attn_ref[...] = jnp.concatenate(outs, axis=1).astype(BF16)

    for c in started:
        c.wait_send()


def on_device(latent, stale_act, stale_kv, gn_gain, gn_bias, temb, conv_w, w_qkv):
    group = lax.axis_index("row") // 4
    lat = latent.reshape(CH, TOK)
    edges = jnp.stack([stale_act[:, 0], stale_act[:, COLS - 1]])
    kv = lax.dynamic_slice_in_dim(stale_kv, group * GC, GC, 1).reshape(2, GC, TOK)
    vm = pl.BlockSpec(memory_space=pltpu.VMEM)
    hbm = pl.BlockSpec(memory_space=pl.ANY)
    scratch = [
        pltpu.VMEM((3, 240, D), BF16),
        pltpu.VMEM((HGROUPS, CH, 3 * GC), BF16),
        pltpu.VMEM((3, 2, 4, 2, CH, 240), BF16),
        pltpu.VMEM((3, 2, 4, CH, 240), BF16),
        pltpu.VMEM((240, 6 * ROWS), BF16),
        pltpu.VMEM((240, 6 * ROWS), BF16),
        pltpu.VMEM((2, CH, ROWS), BF16),
        pltpu.VMEM((8, 128), F32),
        pltpu.VMEM((15, 8, 128), F32),
        pltpu.VMEM((2, 4, CH, TOK), BF16),
        pltpu.VMEM((2, 3, CH, TOK), BF16),
        pltpu.VMEM((CH, TOK), BF16),
        pltpu.VMEM((CH, TOK), BF16),
        pltpu.VMEM((16, CH, TOK), BF16),
        pltpu.VMEM((2, CH, 3 * GC), BF16),
        pltpu.VMEM((16, CH, 3 * GC), BF16),
        pltpu.VMEM((2, 8, GC, TOK), BF16),
        pltpu.VMEM((2, GC, TOK), BF16),
        pltpu.VMEM((QT, GC), BF16),
        pltpu.VMEM((QT, GC), BF16),
        pltpu.VMEM((NHEAD, QT, HEAD), F32),
        pltpu.VMEM((3, QT, 128), BF16),
        pltpu.VMEM((3, QT, 128), BF16),
        pltpu.VMEM((8, 128), F32),
        pltpu.VMEM((8, 128), F32),
        pltpu.VMEM((NHEAD, QT, 128), F32),
        pltpu.SemaphoreType.DMA((NSEM,)),
        pltpu.SemaphoreType.DMA((NSEM,)),
        pltpu.SemaphoreType.DMA((4,)),
    ]
    hid, attn = pl.pallas_call(
        kernel,
        out_shape=(
            jax.ShapeDtypeStruct((CH, TOK), BF16),
            jax.ShapeDtypeStruct((QT, GC), BF16),
        ),
        in_specs=[vm, vm, hbm, vm, vm, vm, hbm, vm],
        out_specs=(vm, vm),
        scratch_shapes=scratch,
        compiler_params=pltpu.CompilerParams(
            collective_id=0, has_side_effects=True, vmem_limit_bytes=56 << 20
        ),
    )(
        lat, edges, kv, gn_gain.reshape(1, CH), gn_bias.reshape(1, CH), temb.reshape(1, CH),
        conv_w.reshape(3, 240, D), w_qkv.transpose(1, 0, 2),
    )
    return hid.reshape(CH, COLS, ROWS), attn.reshape(32, COLS, GC)


def solution(mesh):
    return jax.shard_map(
        on_device,
        mesh=mesh,
        in_specs=(
            P("row", "col", None),
            P("row", "col", None),
            P(None, None, "col", None),
            P("row"),
            P("row"),
            P("row"),
            P(None, None, "row", None),
            P("row", None, None),
        ),
        out_specs=(P("row", "col", None), P("row", "col", None)),
        check_vma=False,
    )
```

time: 664 us -> 76.7 us (0.12)
  waiting for transfers between devices: 483 us -> 0 us
  blocking collectives: 70.6 us -> 0 us
  Pallas kernels: 0 us -> 68.4 us
  local copies, waits for them, and re-layouts: 54.8 us -> 6.85 us
  matrix products: 24.3 us -> 0 us
  between operations: 14.1 us -> 0.7 us
  other arithmetic: 11.9 us -> 0.62 us
    all_gather x3 -> x0, waiting for transfers between devices: 380 us -> none  [the longest x1 210 us: on_device(): lax.all_gather(stale_mine, 'col', axis=2, tiled=True)]
    unnamed x5 -> x0, waiting for transfers between devices: 103 us -> none
    psum x2 -> x0, blocking collectives: 70.6 us -> none  [the longest x1 39.5 us: on_device(): gmean = lax.psum(jnp.sum(grouped, axis=1), 'col') / count]
    pallas_call x0 -> x1, Pallas kernels: none -> 68.4 us  [on_device(): pl.pallas_call(kernel, out_shape=(jax.ShapeDtypeStruct((CH, TOK), BF16),...]
    dot_general x45 -> x0, matrix products: 24.3 us -> none  [the longest x17 7.55 us: attend_block(): jnp.einsum('hdk,hdq->hkq', keys, query, preferred_element_type=jnp.float32)]
    slice x22 -> x1, local copies, waits for them, and re-layouts: 20.8 us -> 0.06 us  [on_device(): edges = jnp.stack([stale_act[:, 0], stale_act[:, COLS - 1]])]
    unnamed x18 -> x7, local copies, waits for them, and re-layouts: 12.1 us -> 2.35 us
    reduce_sum x23 -> x0, other arithmetic: 9.3 us -> none  [the longest x17 3.2 us: attend_block(): total = total * keep + jnp.sum(probs, axis=1)]
  transfers between devices with their start and end apart: 6 -> 0, of which waited for: 4 -> 0; matrix products, arithmetic and copies ran while one was open for 4% -> 0% of each run, Pallas kernels for 0% -> 0%
where the time goes in v1:
time: 76.7 us; the launch traced here: 76.5 us
  Pallas kernels  68.4 us (89%)
  local copies, waits for them, and re-layouts  6.85 us (9%)
    pallas_call x1, Pallas kernels, on_device(): pl.pallas_call(kernel, out_shape=(jax.ShapeDtypeStruct((CH, TOK), BF16),...  68.4 us
    reshape x2, local copies, waits for them, and re-layouts, on_device(): return (hid.reshape(CH, COLS, ROWS), attn.reshape(32, COLS, GC))  3.11 us
    unnamed x7, local copies, waits for them, and re-layouts  2.35 us

profile of v1, /device:TPU:1, one launch (start us, length us, event | category | flops | bytes accessed | tf_op | source)
XLA Modules:
  0.0 76.5 jit_solution(6483507096541725411)
XLA Ops:
  0.6 0.0 copy-start
  0.6 0.0 copy-start.1
  0.7 0.0 copy-start.2
  0.7 1.7 %copy-done = bf16[2,1280,4,128]{3,2,1,0:T(4,128)(2,1)S(1)} copy-done((bf16[2,1280,4,128]{3,2,1,0:T(4,128)(2,1)S(1)}, bf16[2,1280,4,128]{3,2,1,0:T(4,128)(2,1)}, u32[]{:S(2)}) %copy-start) | copy-done | bytes 2621464
  2.4 0.2 constant_dynamic-slice_fusion
  2.6 1.1 %reshape.29.kv_hbm = bf16[2,320,512]{2,1,0:T(8,128)(2,1)} reshape(bf16[2,320,4,128]{3,2,1,0:T(4,128)(2,1)S(1)} %constant_dynamic-slice_fusion) | data formatting | bytes 1310720 | tf_op jit(solution)/shard_map/reshape | solution.py:384
  3.7 0.0 copy-done.1
  3.7 0.1 fusion
  3.8 0.6 pad_maximum_fusion.edge_ref
  4.4 0.0 copy-done.2
  4.4 0.6 copy.20
  5.1 68.4 %shard_map.95 = (bf16[80,512]{1,0:T(8,128)(2,1)}, bf16[128,320]{1,0:T(8,128)(2,1)}) custom-call(bf16[80,512]{1,0:T(8,128)(2,1)} %bitcast.15, bf16[2,80,128]{2,1,0:T(8,128)(2,1)} %pad_maximum_fusion.edge_ref, bf16[2,320,512]{2,1,0:T(8,128)(2,1)} %reshape.29.kv_hbm, f32[1,80]{1,0:T(1,128)} %bitcast.17, f32[1,80]{1,0:T(1,128)} %bitcast.18, f32[1,80]{1,0:T(1,128)} %bitcast.19, ...), custom_call_target="tpu_custom_call" | custom-call | tf_op jit(solution)/shard_map/pallas_call | solution.py:418
  73.4 1.6 %reshape.35 = bf16[32,4,320]{2,1,0:T(4,128)(2,1)} reshape(bf16[128,320]{1,0:T(8,128)(2,1)} %get-tuple-element.5) | data formatting | bytes 163840 | tf_op jit(solution)/shard_map/reshape | solution.py:434
  75.0 1.5 %reshape.34 = bf16[80,4,128]{2,1,0:T(4,128)(2,1)} reshape(bf16[80,512]{1,0:T(8,128)(2,1)} %get-tuple-element.4) | data formatting | bytes 163840 | tf_op jit(solution)/shard_map/reshape | solution.py:434
  (1 shorter events, 0.0 us)
Async XLA Ops:
  0.6 1.7 %copy-start = (bf16[2,1280,4,128]{3,2,1,0:T(4,128)(2,1)S(1)}, bf16[2,1280,4,128]{3,2,1,0:T(4,128)(2,1)}, u32[]{:S(2)}) copy-start(bf16[2,1280,4,128]{3,2,1,0:T(4,128)(2,1)} %param.10) | copy-start | bytes 7864324
  0.6 3.1 %copy-start.1 = (bf16[80,4,128]{2,1,0:T(4,128)(2,1)S(1)}, bf16[80,4,128]{2,1,0:T(4,128)(2,1)}, u32[]{:S(2)}) copy-start(bf16[80,4,128]{2,1,0:T(4,128)(2,1)} %param.9) | copy-start | bytes 245764
  0.7 3.8 %copy-start.2 = (bf16[80,4,128]{2,1,0:T(4,128)(2,1)S(1)}, bf16[80,4,128]{2,1,0:T(4,128)(2,1)}, u32[]{:S(2)}) copy-start(bf16[80,4,128]{2,1,0:T(4,128)(2,1)} %param.8) | copy-start | bytes 245764

commit v2 on v1

--- a/solution.py
+++ b/solution.py
@@ -1,5 +1,4 @@
 import itertools
-import math
 
 import jax
 import jax.numpy as jnp
@@ -25,7 +24,8 @@
 ROWS = 128
 TOK = COLS * ROWS
 QT = 128
-NSEM = 80
+NSEM = 128
+HT = TOK // 2
 
 
 def dot(a, b, ca, cb):
@@ -70,8 +70,8 @@
     nxt = dev(row, (col + 1) % 16)
     prv = dev(row, (col + 15) % 16)
     flip = zl + 1 - 2 * (zl % 2)
-    near = dev(row, y * 4 + flip)
-    qpartner = lpeer[2]
+    near = lpeer[2]
+    qpartner = dev(row, y * 4 + flip)
     others = {
         (dy, dz): dev(row, ((y + dy) % 4) * 4 + (zl + dz) % 4)
         for dy in range(4) for dz in range(4) if dy or dz
@@ -179,8 +179,8 @@
         dlt = t[0:2] - gmean
         gm2 = gm2 + float(n_loc) * dlt * dlt
     ginv = lax.rsqrt(gm2 / float(16 * n_loc) + EPS)
+    c_wz = rcopy(wsrc.at[pl.ds(2 * (1 - zh), 2)], wz, wpeer)
     c_near = rcopy(kv_hbm.at[k], kb.at[k, 4], near)
-    c_wz = rcopy(wsrc.at[pl.ds(2 * (1 - zh), 2)], wz, wpeer)
     c_kvy = {d: rcopy(kv_hbm.at[k], kb.at[k, d], ypeer[d]) for d in (1, 2, 3)}
     mean_c = jnp.concatenate(
         [jnp.broadcast_to(gmean[0:1], (40, 128)), jnp.broadcast_to(gmean[1:2], (40, 128))], axis=0
@@ -196,20 +196,21 @@
 
     c_wt.wait_recv()
     c_x3.wait_recv()
-    c_rx = []
-    for half in range(2):
-        zz = (1 - zh) if half == 0 else zh
-        acc = jnp.zeros((4 * CH, TOK), F32)
-        for a in range(3):
-            acc = acc + dot(
-                wt[a, zz, :, k].reshape(4 * CH, 240), x3[:, a * ROWS:a * ROWS + TOK], 1, 0
-            )
-        for a in range(3):
-            acc = acc + dot(
-                wtsib[a, zz].reshape(4 * CH, 240), x3sib[:, a * ROWS:a * ROWS + TOK], 1, 0
-            )
-        pb[half] = acc.astype(BF16).reshape(4, CH, TOK)
-        c_rx.append([rcopy(pb.at[half, xs[d]], rx.at[half, d - 1], xpeer[d]) for d in (1, 2, 3)])
+    c_rx = {}
+    for t in range(2):
+        for half in range(2):
+            zz = (1 - zh) if half == 0 else zh
+            acc = jnp.zeros((4 * CH, HT), F32)
+            for wv, xv in ((wt.at[:, :, :, k], x3), (wtsib, x3sib)):
+                for a in range(3):
+                    first = a * ROWS + t * HT
+                    acc = acc + dot(
+                        wv[a, zz].reshape(4 * CH, 240), xv[:, first:first + HT], 1, 0
+                    )
+            pb[t, half] = acc.astype(BF16).reshape(4, CH, HT)
+            c_rx[t, half] = [
+                rcopy(pb.at[t, half, xs[d]], rx.at[t, half, d - 1], xpeer[d]) for d in (1, 2, 3)
+            ]
 
     def keys_second():
         c_near.wait_recv()
@@ -224,32 +225,40 @@
         cx = {d: rcopy(wz.at[xs[d] // 2], wg.at[r_z], xpeer[d]) for d in (1, 2, 3)}
         return lc, cx, rcopy(wz.at[mine], wg.at[r_z], sib)
 
-    sums = []
-    for half in range(2):
-        for c in c_rx[half]:
-            c.wait_recv()
-        total = pb[half, x].astype(F32)
+    def collect(t, half):
+        total = pb[t, half, x].astype(F32)
         for d in range(3):
-            total = total + rx[half, d].astype(F32)
-        if half == 0:
-            zs[...] = total.astype(BF16)
-            c_zr = rcopy(zs, zr, zpeer)
-        sums.append(total)
-
+            c_rx[t, half][d].wait_recv()
+            total = total + rx[t, half, d].astype(F32)
+        return total
+
+    def block(r, t):
+        return hall.at[r, :, pl.ds(t * HT, HT)]
+
+    def residual(t, own):
+        c_zr[t].wait_recv()
+        lanes = slice(t * HT, (t + 1) * HT)
+        hid = (xf[:, lanes] + (own + zr[t].astype(F32)) + temb).astype(BF16)
+        hid_ref[:, lanes] = hid
+        hall[row, :, lanes] = hid
+        c_hz.append(rcopy(block(row, t), block(row, t), zpeer))
+        c_hx[t] = {d: rcopy(block(row, t), block(row, t), xpeer[d]) for d in (1, 2, 3)}
+        c_hs.append(rcopy(block(row, t), block(row, t), sib))
+
+    c_zr, c_hz, c_hx, c_hx2, c_hs = [], [], {}, {}, []
+    own = []
+    for t in range(2):
+        zs[t] = collect(t, 0).astype(BF16)
+        c_zr.append(rcopy(zs.at[t], zr.at[t], zpeer))
+        own.append(collect(t, 1))
+    lc_z, c_wx2, c_ws2 = weights_second()
     c_kvy2, c_ks = keys_second()
-    lc_z, c_wx2, c_ws2 = weights_second()
-
-    c_zr.wait_recv()
-    hid = (xf + (sums[1] + zr[...].astype(F32)) + temb).astype(BF16)
-    hid_ref[...] = hid
-    hall[row] = hid
-
-    c_hz = rcopy(hall.at[row], hall.at[row], zpeer)
-    c_hx = {d: rcopy(hall.at[row], hall.at[row], xpeer[d]) for d in (1, 2, 3)}
-    c_hs = [rcopy(hall.at[row], hall.at[row], sib)]
-    c_hz.wait_recv()
-    c_hx2 = {d: rcopy(hall.at[r_z], hall.at[r_z], xpeer[d]) for d in (1, 2, 3)}
-    c_hs.append(rcopy(hall.at[r_z], hall.at[r_z], sib))
+    residual(0, own[0])
+    residual(1, own[1])
+    for t in range(2):
+        c_hz[t].wait_recv()
+        c_hx2[t] = {d: rcopy(block(r_z, t), block(r_z, t), xpeer[d]) for d in (1, 2, 3)}
+        c_hs.append(rcopy(block(r_z, t), block(r_z, t), sib))
 
     w_fwd = []
     for d in (1, 2, 3):
@@ -259,10 +268,11 @@
         c_kvy[d].wait_recv()
         c_ks.append(rcopy(kb.at[k, d], kb.at[k, d], sib))
     for leg, cs in ((0, c_hx), (1, c_hx2)):
-        for d in (1, 2, 3):
-            src = at_row(zh if leg == 0 else 1 - zh, (x + 4 - d) % 4, k)
-            cs[d].wait_recv()
-            c_hs.append(rcopy(hall.at[src], hall.at[src], sib))
+        for t in range(2):
+            for d in (1, 2, 3):
+                src = at_row(zh if leg == 0 else 1 - zh, (x + 4 - d) % 4, k)
+                cs[t][d].wait_recv()
+                c_hs.append(rcopy(block(src, t), block(src, t), sib))
     for d in (1, 2, 3):
         src = at_row(1 - zh, (x + 4 - d) % 4, k)
         c_wx2[d].wait_recv()
@@ -289,7 +299,7 @@
     rstd = lax.rsqrt(nvar + EPS)
     proj = dot(wfull, hfull, 0, 0)
     qkv = (proj - colsum[:, 0:1] * mu) * rstd
-    qcm = (qkv[0:GC] * (HEAD ** -0.5 * math.log2(math.e))).astype(BF16)
+    qcm = (qkv[0:GC] * HEAD ** -0.5).astype(BF16)
     kf[0] = qkv[GC:2 * GC].astype(BF16)
     kf[1] = qkv[2 * GC:].astype(BF16)
 
@@ -318,10 +328,10 @@
     def weigh(scores, best, values):
         out = jnp.zeros((QT, HEAD + 16), F32)
         for s, v in zip(scores, values):
-            p = jnp.exp2(s - best).astype(BF16)
+            p = jnp.exp(s - best).astype(BF16)
             out = out + dot(p, jnp.concatenate([v, jnp.ones((16, TOK), BF16)], axis=0), 1, 1)
         norm = out[:, HEAD:HEAD + 1]
-        return out[:, 0:HEAD] / norm, best + jnp.log2(norm)
+        return out[:, 0:HEAD] / norm, best + jnp.log(norm)
 
     diag = lax.broadcasted_iota(jnp.int32, (QT, QT), 0) == lax.broadcasted_iota(jnp.int32, (QT, QT), 1)
     c_o = []
@@ -368,13 +378,19 @@
         lse1 = as_column(lback[h:h + 1])
         lse0 = lses[h][:, 0:1]
         top = jnp.maximum(lse0, lse1)
-        w0 = jnp.exp2(lse0 - top)
-        w1 = jnp.exp2(lse1 - top)
+        w0 = jnp.exp(lse0 - top)
+        w1 = jnp.exp(lse1 - top)
         outs.append((oown[h] * w0 + o1 * w1) / (w0 + w1))
     attn_ref[...] = jnp.concatenate(outs, axis=1).astype(BF16)
 
     for c in started:
         c.wait_send()
+
+
+def place(h_ref, a_ref, hid_ref, attn_ref):
+    for w in range(COLS):
+        hid_ref[:, w, :] = h_ref[:, w * ROWS:(w + 1) * ROWS]
+    attn_ref[...] = a_ref[...].reshape(32, COLS, GC)
 
 
 def on_device(latent, stale_act, stale_kv, gn_gain, gn_bias, temb, conv_w, w_qkv):
@@ -394,10 +410,10 @@
         pltpu.VMEM((2, CH, ROWS), BF16),
         pltpu.VMEM((8, 128), F32),
         pltpu.VMEM((15, 8, 128), F32),
-        pltpu.VMEM((2, 4, CH, TOK), BF16),
-        pltpu.VMEM((2, 3, CH, TOK), BF16),
-        pltpu.VMEM((CH, TOK), BF16),
-        pltpu.VMEM((CH, TOK), BF16),
+        pltpu.VMEM((2, 2, 4, CH, HT), BF16),
+        pltpu.VMEM((2, 2, 3, CH, HT), BF16),
+        pltpu.VMEM((2, CH, HT), BF16),
+        pltpu.VMEM((2, CH, HT), BF16),
         pltpu.VMEM((16, CH, TOK), BF16),
         pltpu.VMEM((2, CH, 3 * GC), BF16),
         pltpu.VMEM((16, CH, 3 * GC), BF16),
@@ -431,7 +447,15 @@
         lat, edges, kv, gn_gain.reshape(1, CH), gn_bias.reshape(1, CH), temb.reshape(1, CH),
         conv_w.reshape(3, 240, D), w_qkv.transpose(1, 0, 2),
     )
-    return hid.reshape(CH, COLS, ROWS), attn.reshape(32, COLS, GC)
+    return pl.pallas_call(
+        place,
+        out_shape=(
+            jax.ShapeDtypeStruct((CH, COLS, ROWS), BF16),
+            jax.ShapeDtypeStruct((32, COLS, GC), BF16),
+        ),
+        in_specs=[vm, vm],
+        out_specs=(vm, vm),
+    )(hid, attn)
 
 
 def solution(mesh):

time: 76.7 us -> 73.8 us (0.962)
  local copies, waits for them, and re-layouts: 6.85 us -> 3.74 us
    reshape x2 -> x0, local copies, waits for them, and re-layouts: 3.11 us -> none  [on_device(): return (hid.reshape(CH, COLS, ROWS), attn.reshape(32, COLS, GC))]
    pallas_call x0 -> x1, Pallas kernels: none -> 1.88 us  [on_device(): pl.pallas_call(place, out_shape=(jax.ShapeDtypeStruct((CH, COLS, ROWS), B...]
    pallas_call x1, Pallas kernels: 68.4 us -> 66.7 us  [on_device(): pl.pallas_call(kernel, out_shape=(jax.ShapeDtypeStruct((CH, TOK), BF16),...]
where the time goes in v2:
time: 73.8 us; the launch traced here: 73.6 us
  Pallas kernels  68.6 us (93%)
  local copies, waits for them, and re-layouts  3.74 us (5%)
    pallas_call x1, Pallas kernels, on_device(): pl.pallas_call(kernel, out_shape=(jax.ShapeDtypeStruct((CH, TOK), BF16),...  66.7 us
    unnamed x7, local copies, waits for them, and re-layouts  2.35 us
    pallas_call x1, Pallas kernels, on_device(): pl.pallas_call(place, out_shape=(jax.ShapeDtypeStruct((CH, COLS, ROWS), B...  1.88 us

profile of v2, /device:TPU:1, one launch (start us, length us, event | category | flops | bytes accessed | tf_op | source)
XLA Modules:
  0.0 73.6 jit_solution(8161545002494425668)
XLA Ops:
  0.6 0.0 copy-start
  0.6 0.0 copy-start.1
  0.7 0.0 copy-start.2
  0.7 1.7 %copy-done = bf16[2,1280,4,128]{3,2,1,0:T(4,128)(2,1)S(1)} copy-done((bf16[2,1280,4,128]{3,2,1,0:T(4,128)(2,1)S(1)}, bf16[2,1280,4,128]{3,2,1,0:T(4,128)(2,1)}, u32[]{:S(2)}) %copy-start) | copy-done | bytes 2621464
  2.4 0.2 constant_dynamic-slice_fusion
  2.6 1.1 %reshape.23.kv_hbm = bf16[2,320,512]{2,1,0:T(8,128)(2,1)} reshape(bf16[2,320,4,128]{3,2,1,0:T(4,128)(2,1)S(1)} %constant_dynamic-slice_fusion) | data formatting | bytes 1310720 | tf_op jit(solution)/shard_map/reshape | solution.py:400
  3.7 0.0 copy-done.1
  3.7 0.1 fusion
  3.8 0.6 pad_maximum_fusion.edge_ref
  4.4 0.0 copy-done.2
  4.4 0.6 copy.18
  5.1 66.7 %shard_map.95 = (bf16[80,512]{1,0:T(8,128)(2,1)}, bf16[128,320]{1,0:T(8,128)(2,1)}) custom-call(bf16[80,512]{1,0:T(8,128)(2,1)} %bitcast.15, bf16[2,80,128]{2,1,0:T(8,128)(2,1)} %pad_maximum_fusion.edge_ref, bf16[2,320,512]{2,1,0:T(8,128)(2,1)} %reshape.23.kv_hbm, f32[1,80]{1,0:T(1,128)} %bitcast.17, f32[1,80]{1,0:T(1,128)} %bitcast.18, f32[1,80]{1,0:T(1,128)} %bitcast.19, ...), custom_call_target="tpu_custom_call" | custom-call | tf_op jit(solution)/shard_map/pallas_call | solution.py:434
  71.7 1.9 %shard_map.96 = (bf16[80,4,128]{2,1,0:T(4,128)(2,1)}, bf16[32,4,320]{2,1,0:T(4,128)(2,1)}) custom-call(bf16[80,512]{1,0:T(8,128)(2,1)} %get-tuple-element.4.h_ref, bf16[128,320]{1,0:T(8,128)(2,1)} %get-tuple-element.5.a_ref), custom_call_target="tpu_custom_call" | custom-call | tf_op jit(solution)/shard_map/pallas_call | solution.py:450
  (1 shorter events, 0.0 us)
Async XLA Ops:
  0.6 1.7 %copy-start = (bf16[2,1280,4,128]{3,2,1,0:T(4,128)(2,1)S(1)}, bf16[2,1280,4,128]{3,2,1,0:T(4,128)(2,1)}, u32[]{:S(2)}) copy-start(bf16[2,1280,4,128]{3,2,1,0:T(4,128)(2,1)} %param.10) | copy-start | bytes 7864324
  0.6 3.1 %copy-start.1 = (bf16[80,4,128]{2,1,0:T(4,128)(2,1)S(1)}, bf16[80,4,128]{2,1,0:T(4,128)(2,1)}, u32[]{:S(2)}) copy-start(bf16[80,4,128]{2,1,0:T(4,128)(2,1)} %param.9) | copy-start | bytes 245764
  0.7 3.8 %copy-start.2 = (bf16[80,4,128]{2,1,0:T(4,128)(2,1)S(1)}, bf16[80,4,128]{2,1,0:T(4,128)(2,1)}, u32[]{:S(2)}) copy-start(bf16[80,4,128]{2,1,0:T(4,128)(2,1)} %param.8) | copy-start | bytes 245764

commit v3 on v2

--- a/solution.py
+++ b/solution.py
@@ -40,9 +40,9 @@
 
 
 def kernel(
-    lat_ref, edge_ref, kv_hbm, gain_ref, bias_ref, temb_ref, cw_hbm, w_ref,
+    lat_ref, act_ref, kv_hbm, gain_ref, bias_ref, temb_ref, cw_hbm, w_ref,
     hid_ref, attn_ref,
-    cw, wsrc, wt, wtsib, x3, x3sib, halo, st_a, st_all, pb, rx, zs, zr,
+    cw, edge, wsrc, wt, wtsib, x3, x3sib, halo, st_a, st_all, pb, rx, zs, zr,
     hall, wz, wg, kb, kf, qx, qpeer, oown, oret, oback, lret, lback, lses,
     ss, rs, ls,
 ):
@@ -107,7 +107,7 @@
     lc_own = pltpu.make_async_copy(wsrc.at[group], wg.at[row], ls.at[2])
     lc_own.start()
 
-    xf = lat_ref[...].astype(F32)
+    xf = jnp.concatenate([lat_ref[:, w, :].astype(F32) for w in range(COLS)], axis=1)
     n_loc = 40 * TOK
     halves = [xf[0:40], xf[40:80]]
     means = [jnp.sum(jnp.sum(h, axis=1, keepdims=True), axis=0, keepdims=True) / n_loc for h in halves]
@@ -121,13 +121,16 @@
         tile = jnp.where(rid == i, jnp.broadcast_to(v, (8, 128)), tile)
     st_a[...] = tile
 
+    edge[0] = act_ref[:, 0, :]
+    edge[1] = act_ref[:, COLS - 1, :]
+
     pl.semaphore_wait(bar, len(peers))
 
     c_st = [
         rcopy(st_a, st_all.at[dy * 4 + dz - 1], to) for (dy, dz), to in others.items()
     ]
-    c_halo_n = rcopy(edge_ref.at[1], halo.at[0], nxt)
-    c_halo_p = rcopy(edge_ref.at[0], halo.at[1], prv)
+    c_halo_n = rcopy(edge.at[1], halo.at[0], nxt)
+    c_halo_p = rcopy(edge.at[0], halo.at[1], prv)
 
     c_wx = {d: rcopy(wsrc.at[zh * 2 + xs[d] // 2], wg.at[row], xpeer[d]) for d in (1, 2, 3)}
     c_ws = rcopy(wsrc.at[group], wg.at[row], sib)
@@ -395,13 +398,12 @@
 
 def on_device(latent, stale_act, stale_kv, gn_gain, gn_bias, temb, conv_w, w_qkv):
     group = lax.axis_index("row") // 4
-    lat = latent.reshape(CH, TOK)
-    edges = jnp.stack([stale_act[:, 0], stale_act[:, COLS - 1]])
     kv = lax.dynamic_slice_in_dim(stale_kv, group * GC, GC, 1).reshape(2, GC, TOK)
     vm = pl.BlockSpec(memory_space=pltpu.VMEM)
     hbm = pl.BlockSpec(memory_space=pl.ANY)
     scratch = [
         pltpu.VMEM((3, 240, D), BF16),
+        pltpu.VMEM((2, CH, ROWS), BF16),
         pltpu.VMEM((HGROUPS, CH, 3 * GC), BF16),
         pltpu.VMEM((3, 2, 4, 2, CH, 240), BF16),
         pltpu.VMEM((3, 2, 4, CH, 240), BF16),
@@ -444,7 +446,7 @@
             collective_id=0, has_side_effects=True, vmem_limit_bytes=56 << 20
         ),
     )(
-        lat, edges, kv, gn_gain.reshape(1, CH), gn_bias.reshape(1, CH), temb.reshape(1, CH),
+        latent, stale_act, kv, gn_gain.reshape(1, CH), gn_bias.reshape(1, CH), temb.reshape(1, CH),
         conv_w.reshape(3, 240, D), w_qkv.transpose(1, 0, 2),
     )
     return pl.pallas_call(

time: 73.8 us -> 72.4 us (0.981)
    unnamed x7 -> x2, local copies, waits for them, and re-layouts: 2.35 us -> 1.72 us
where the time goes in v3:
time: 72.4 us; the launch traced here: 72.3 us
  Pallas kernels  68.6 us (95%)
  local copies, waits for them, and re-layouts  3.04 us (4%)
    pallas_call x1, Pallas kernels, on_device(): pl.pallas_call(kernel, out_shape=(jax.ShapeDtypeStruct((CH, TOK), BF16),...  66.7 us
    pallas_call x1, Pallas kernels, on_device(): pl.pallas_call(place, out_shape=(jax.ShapeDtypeStruct((CH, COLS, ROWS), B...  1.88 us
    unnamed x2, local copies, waits for them, and re-layouts  1.72 us

profile of v3, /device:TPU:1, one launch (start us, length us, event | category | flops | bytes accessed | tf_op | source)
XLA Modules:
  0.0 72.3 jit_solution(9347870441633663518)
XLA Ops:
  0.6 0.0 copy-start
  0.7 1.7 %copy-done = bf16[2,1280,4,128]{3,2,1,0:T(4,128)(2,1)S(1)} copy-done((bf16[2,1280,4,128]{3,2,1,0:T(4,128)(2,1)S(1)}, bf16[2,1280,4,128]{3,2,1,0:T(4,128)(2,1)}, u32[]{:S(2)}) %copy-start) | copy-done | bytes 2621464
  2.4 0.2 constant_dynamic-slice_fusion
  2.6 1.1 %reshape.19.kv_hbm = bf16[2,320,512]{2,1,0:T(8,128)(2,1)} reshape(bf16[2,320,4,128]{3,2,1,0:T(4,128)(2,1)S(1)} %constant_dynamic-slice_fusion) | data formatting | bytes 1310720 | tf_op jit(solution)/shard_map/reshape | solution.py:401
  3.7 66.7 %shard_map.95 = (bf16[80,512]{1,0:T(8,128)(2,1)}, bf16[128,320]{1,0:T(8,128)(2,1)}) custom-call(bf16[80,4,128]{2,1,0:T(4,128)(2,1)} %lat_ref.1, bf16[80,4,128]{2,1,0:T(4,128)(2,1)} %act_ref.1, bf16[2,320,512]{2,1,0:T(8,128)(2,1)} %reshape.19.kv_hbm, f32[1,80]{1,0:T(1,128)} %bitcast.7, f32[1,80]{1,0:T(1,128)} %bitcast.8, f32[1,80]{1,0:T(1,128)} %bitcast.9, ...), custom_call_target="tpu_custom_call" | custom-call | tf_op jit(solution)/shard_map/pallas_call | solution.py:436
  70.4 1.9 %shard_map.96 = (bf16[80,4,128]{2,1,0:T(4,128)(2,1)}, bf16[32,4,320]{2,1,0:T(4,128)(2,1)}) custom-call(bf16[80,512]{1,0:T(8,128)(2,1)} %get-tuple-element.4.h_ref, bf16[128,320]{1,0:T(8,128)(2,1)} %get-tuple-element.5.a_ref), custom_call_target="tpu_custom_call" | custom-call | tf_op jit(solution)/shard_map/pallas_call | solution.py:452
Async XLA Ops:
  0.6 1.7 %copy-start = (bf16[2,1280,4,128]{3,2,1,0:T(4,128)(2,1)S(1)}, bf16[2,1280,4,128]{3,2,1,0:T(4,128)(2,1)}, u32[]{:S(2)}) copy-start(bf16[2,1280,4,128]{3,2,1,0:T(4,128)(2,1)} %param.10) | copy-start | bytes 7864324

commit v4 on v3

--- a/solution.py
+++ b/solution.py
@@ -281,10 +281,6 @@
         c_wx2[d].wait_recv()
         w_fwd.append(rcopy(wg.at[src], wg.at[src], sib))
 
-    c_kfwd = []
-    for d in (1, 2, 3):
-        c_kvy2[d].wait_recv()
-        c_kfwd.append(rcopy(kb.at[k, 4 + d], kb.at[k, 4 + d], sib))
 
     lc_own.wait()
     lc_z.wait()
@@ -294,6 +290,11 @@
     colsum = dot(wfull, jnp.ones((D, 128), BF16), 0, 0)
     for c in c_hs:
         c.wait_recv()
+
+    c_kfwd = []
+    for d in (1, 2, 3):
+        c_kvy2[d].wait_recv()
+        c_kfwd.append(rcopy(kb.at[k, 4 + d], kb.at[k, 4 + d], sib))
 
     hfull = hall[...].reshape(D, TOK)
     hf = hfull.astype(F32)

time: 72.4 us -> 73.2 us (1.011)
  no operation moved by 1% of the time
where the time goes in v4:
time: 73.2 us; the launch traced here: 72.9 us
  Pallas kernels  69.2 us (95%)
  local copies, waits for them, and re-layouts  3.04 us (4%)
    pallas_call x1, Pallas kernels, on_device(): pl.pallas_call(kernel, out_shape=(jax.ShapeDtypeStruct((CH, TOK), BF16),...  67.3 us
    pallas_call x1, Pallas kernels, on_device(): pl.pallas_call(place, out_shape=(jax.ShapeDtypeStruct((CH, COLS, ROWS), B...  1.88 us
    unnamed x2, local copies, waits for them, and re-layouts  1.72 us

profile of v4, /device:TPU:1, one launch (start us, length us, event | category | flops | bytes accessed | tf_op | source)
XLA Modules:
  0.0 72.9 jit_solution(9305486330990220329)
XLA Ops:
  0.6 0.0 copy-start
  0.7 1.7 %copy-done = bf16[2,1280,4,128]{3,2,1,0:T(4,128)(2,1)S(1)} copy-done((bf16[2,1280,4,128]{3,2,1,0:T(4,128)(2,1)S(1)}, bf16[2,1280,4,128]{3,2,1,0:T(4,128)(2,1)}, u32[]{:S(2)}) %copy-start) | copy-done | bytes 2621464
  2.4 0.2 constant_dynamic-slice_fusion
  2.6 1.1 %reshape.19.kv_hbm = bf16[2,320,512]{2,1,0:T(8,128)(2,1)} reshape(bf16[2,320,4,128]{3,2,1,0:T(4,128)(2,1)S(1)} %constant_dynamic-slice_fusion) | data formatting | bytes 1310720 | tf_op jit(solution)/shard_map/reshape | solution.py:402
  3.7 67.3 %shard_map.95 = (bf16[80,512]{1,0:T(8,128)(2,1)}, bf16[128,320]{1,0:T(8,128)(2,1)}) custom-call(bf16[80,4,128]{2,1,0:T(4,128)(2,1)} %lat_ref.1, bf16[80,4,128]{2,1,0:T(4,128)(2,1)} %act_ref.1, bf16[2,320,512]{2,1,0:T(8,128)(2,1)} %reshape.19.kv_hbm, f32[1,80]{1,0:T(1,128)} %bitcast.7, f32[1,80]{1,0:T(1,128)} %bitcast.8, f32[1,80]{1,0:T(1,128)} %bitcast.9, ...), custom_call_target="tpu_custom_call" | custom-call | tf_op jit(solution)/shard_map/pallas_call | solution.py:437
  71.0 1.9 %shard_map.96 = (bf16[80,4,128]{2,1,0:T(4,128)(2,1)}, bf16[32,4,320]{2,1,0:T(4,128)(2,1)}) custom-call(bf16[80,512]{1,0:T(8,128)(2,1)} %get-tuple-element.4.h_ref, bf16[128,320]{1,0:T(8,128)(2,1)} %get-tuple-element.5.a_ref), custom_call_target="tpu_custom_call" | custom-call | tf_op jit(solution)/shard_map/pallas_call | solution.py:453
Async XLA Ops:
  0.6 1.7 %copy-start = (bf16[2,1280,4,128]{3,2,1,0:T(4,128)(2,1)S(1)}, bf16[2,1280,4,128]{3,2,1,0:T(4,128)(2,1)}, u32[]{:S(2)}) copy-start(bf16[2,1280,4,128]{3,2,1,0:T(4,128)(2,1)} %param.10) | copy-start | bytes 7864324
